TPU v7x, 256 devices: a whole 4x4x8 slice. The times are simulated.
256 devices in a mesh: depth: 8 (over z), row: 4 (over y), col: 8 (over x, core).
Axes of the slice: x: 4, y: 4, z: 8, core: 2. Of those that a mesh axis runs over, the one named last changes fastest.
Arguments:
- density: bfloat16 [64, 512, 2048], P('depth', 'row', 'col'), may hold values from 0.0046691895 to 0.09375
- emission: bfloat16 [3, 64, 512, 2048], P(None, 'depth', 'row', 'col'), may hold values from 0.19921875 to 5
- offsets: int32 [3, 2, 8, 4, 16], P(None, None, 'depth', 'row', 'col'), may hold values from -8 to 8
- view_order: int32 [3, 4], P(None, 'row'), may hold values from 0 to 1
Outputs:
- image: float32 [3, 4, 64, 8, 2048], P(None, None, 'row', 'depth', 'col')
Inputs may be any that keep to these rules, and one draw needn't show every extreme that they name: `offsets`: displacement in cells of each brick's footprint from its home position in each view. `view_order`: 1 reverses the rays' direction along depth in that view and band of brick rows.
All inputs are finite; a program needn't handle non-finite values.
Results may differ from a plain program's by a relative error of at most 0.00052.
Values sent between devices are 32-bit elements; how exact they have to be, the bound alone decides.
A program may use at most 128 MiB of HBM per device.

v0:
```python
import jax
import jax.numpy as jnp
from jax import lax
from jax.sharding import PartitionSpec as P

MARGIN = 16
JIT = 8
VIEWS = 3


SHEAR_ROWS = (0.75, -0.5, 0.25)
SHEAR_COLS = (-0.25, 0.625, -0.875)


def partner(block, axis, stride):
    count = lax.axis_size(axis)
    route = []
    for low in range(count):
        high = low | 1 << stride
        if high != low and high < count:
            route += [(low, high), (high, low)]
    return lax.ppermute(block, axis, route)


def extended(block, sides, width):
    for axis, dim in sides:
        count = lax.axis_size(axis)
        forward = [(i, i + 1) for i in range(count - 1)]
        forward.append((count - 1, 0))
        backward = [(target, source) for source, target in forward]
        low = lax.ppermute(
            lax.slice_in_dim(block, block.shape[dim] - width, None, axis=dim), axis, forward
        )
        high = lax.ppermute(lax.slice_in_dim(block, 0, width, axis=dim), axis, backward)
        block = jnp.concatenate([low, block, high], axis=dim)
    return block


def bilinear(shear_rate, slices, length, margin):
    tile_width = length + 2 * margin
    slice_pos = jnp.arange(slices, dtype=jnp.float32)
    slice_shift = shear_rate * (margin - 2) * (2.0 * slice_pos - (slices - 1)) / slices
    target = jnp.arange(tile_width, dtype=jnp.float32)
    source = jnp.arange(length, dtype=jnp.float32)
    distance = target[None, :, None] - margin - slice_shift[:, None, None] - source[None, None, :]
    return jnp.maximum(0.0, 1.0 - jnp.abs(distance)).astype(jnp.bfloat16)


def integrate(footprint, backward):
    extinction = footprint[0]
    running = jnp.cumsum(extinction, axis=-3)
    total_depth = jnp.sum(extinction, axis=-3)
    prefix_depth = jnp.where(backward, total_depth[..., None, :, :] - running, running - extinction)
    weight = (1.0 - jnp.exp(-extinction)) * jnp.exp(-prefix_depth)
    colors = jnp.sum(footprint[1:] * weight, axis=-3)
    return jnp.concatenate([colors, total_depth[None]], 0)


def pad_along(source_array, lead_count, trail_count, axis_pos):
    widths = [(0, 0)] * source_array.ndim
    widths[axis_pos] = (lead_count, trail_count)
    return jnp.pad(source_array, widths)


def fold_rims(padded, rim_width, cell_count, axis_pos):
    interior = lax.slice_in_dim(padded, 2 * rim_width, 2 * rim_width + cell_count, axis=axis_pos)
    from_above = lax.slice_in_dim(padded, 0, rim_width, axis=axis_pos)
    from_below = lax.slice_in_dim(
        padded, cell_count + 3 * rim_width, cell_count + 4 * rim_width, axis=axis_pos
    )
    return (
        interior
        + pad_along(from_above, 0, cell_count - rim_width, axis_pos)
        + pad_along(from_below, cell_count - rim_width, 0, axis_pos)
    )


def render_view(fields, view_index, offsets, backward):
    slices = fields.shape[1]
    length = fields.shape[2]
    bricks = fields.shape[3]
    row_weights = bilinear(SHEAR_ROWS[view_index], slices, length, MARGIN)
    col_weights = bilinear(SHEAR_COLS[view_index], slices, length, MARGIN)
    resampled = jnp.einsum(
        "fzybx,zux->fzybu", fields, col_weights, preferred_element_type=jnp.float32
    ).astype(jnp.bfloat16)
    footprint = jnp.einsum(
        "zty,fzybu->fbztu", row_weights, resampled, preferred_element_type=jnp.float32
    )
    shaded = integrate(footprint, backward)
    rim_width = MARGIN + JIT
    tile_width = length + 2 * MARGIN
    canvas = jnp.zeros((4, length + 2 * rim_width, bricks * length + 2 * rim_width), jnp.float32)
    for brick_index in range(bricks):
        top_row = offsets[view_index, 0, 0, 0, brick_index] + JIT
        left_col = offsets[view_index, 1, 0, 0, brick_index] + brick_index * length + JIT
        corner = (jnp.int32(0), top_row, left_col)
        current = lax.dynamic_slice(canvas, corner, (4, tile_width, tile_width))
        canvas = lax.dynamic_update_slice(canvas, current + shaded[:, brick_index], corner)
    return canvas


def over_combine(front_part, back_part):
    screen = jnp.exp(-front_part[:, 3:4])
    colors = front_part[:, :3] + screen * back_part[:, :3]
    return jnp.concatenate([colors, front_part[:, 3:4] + back_part[:, 3:4]], 1)


def composite(owned, orders):
    view_count, channels, length, columns = owned.shape
    sections = lax.axis_size("depth")
    phase_rows = length // sections
    backward = (orders == 1)[:, None, None, None, None]
    current = owned.reshape(view_count, channels, phase_rows, sections, columns)
    position = lax.axis_index("depth")
    for section_bit in range(sections.bit_length() - 1):
        paired = current.reshape(
            view_count, channels, phase_rows, current.shape[3] // 2, 2, columns
        )
        mine_bit = position >> section_bit & 1
        lower_half = paired[:, :, :, :, 0]
        upper_half = paired[:, :, :, :, 1]
        kept_half = jnp.where(mine_bit == 0, lower_half, upper_half)
        given_half = jnp.where(mine_bit == 0, upper_half, lower_half)
        received = partner(given_half, "depth", section_bit)
        mine_front = jnp.logical_xor(mine_bit == 0, backward)
        front_part = jnp.where(mine_front, kept_half, received)
        back_part = jnp.where(mine_front, received, kept_half)
        current = over_combine(front_part, back_part)
    colors = current[:, :3]
    depth_sum = current[:, 3:4]
    return jnp.concatenate([colors, jnp.exp(-depth_sum)], 1)


def spill_and_composite(canvases, orders, length, columns):
    rim_width = MARGIN + JIT
    padded = extended(canvases, (("row", 2), ("col", 3)), rim_width)
    owned = fold_rims(fold_rims(padded, rim_width, length, 2), rim_width, columns, 3)
    return composite(owned, orders)


def local(density, emission, offsets, view_order):
    slices, length, columns = density.shape
    bricks = columns // length
    band_orders = view_order[:, 0]
    fields = jnp.concatenate([density[None], emission], 0).reshape(
        4, slices, length, bricks, length
    )
    canvases = jnp.stack(
        [
            render_view(fields, view_index, offsets, band_orders[view_index] == 1)
            for view_index in range(VIEWS)
        ]
    )
    return spill_and_composite(canvases, band_orders, length, columns)


def solution(mesh):
    return jax.shard_map(
        local,
        mesh=mesh,
        in_specs=(
            P("depth", "row", "col"),
            P(None, "depth", "row", "col"),
            P(None, None, "depth", "row", "col"),
            P(None, "row"),
        ),
        out_specs=P(None, None, "row", "depth", "col"),
        check_vma=False,
    )
```

profile of v0, /device:TPU:6, one launch (start us, length us, event | category | flops | bytes accessed | tf_op | source)
XLA Modules:
  0.0 233.5 jit_solution(13974833472751469198)
XLA Ops:
  4.6 5.2 %convolution_bitcast_fusion.2 = f32[4,2,8,160,160]{3,4,1,0,2:T(8,128)} fusion(bf16[3,8,128,2,128]{4,2,3,0,1:T(8,128)(2,1)S(1)} %copy.68, bf16[1,8,128,2,128]{4,2,3,0,1:T(8,128)(2,1)S(1)} %copy.67, f32[8,160]{1,0:T(8,128)S(1)} %get-tuple-element.34, f32[8,160]{1,0:T(8,128)S(1)} %get-tuple-element.33), kind=kOutput, calls=%fused_computation.10 | convolution fusion | flops 762118144 | bytes 8660992 | tf_op jit(solution)/shard_map/zty,fzybu->fbztu/dot_general | solution.py:87
  11.8 3.5 %fusion.19 = f32[1,2,8,160,160]{3,4,1,0,2:T(8,128)} fusion(f32[4,2,8,160,160]{3,4,1,0,2:T(8,128)} %convolution_bitcast_fusion.2), kind=kOutput, calls=%fused_computation.29 | output fusion | flops 2867200 | bytes 4259840 | tf_op jit(solution)/shard_map/jit(cumsum)/reduce_window_sum | solution.py:51
  18.5 5.1 %convolution_bitcast_fusion.1 = f32[4,2,8,160,160]{3,4,1,0,2:T(8,128)} fusion(bf16[3,8,128,2,128]{4,2,3,0,1:T(8,128)(2,1)S(1)} %copy.68, bf16[1,8,128,2,128]{4,2,3,0,1:T(8,128)(2,1)S(1)} %copy.67, f32[8,160]{1,0:T(8,128)S(1)} %get-tuple-element.36, f32[8,160]{1,0:T(8,128)S(1)} %get-tuple-element.35), kind=kOutput, calls=%fused_computation.9 | convolution fusion | flops 762118144 | bytes 8660992 | tf_op jit(solution)/shard_map/zty,fzybu->fbztu/dot_general | solution.py:87
  25.5 3.5 %fusion.17 = f32[1,2,8,160,160]{3,4,1,0,2:T(8,128)} fusion(f32[4,2,8,160,160]{3,4,1,0,2:T(8,128)} %convolution_bitcast_fusion.1), kind=kOutput, calls=%fused_computation.26 | output fusion | flops 2867200 | bytes 4259840 | tf_op jit(solution)/shard_map/jit(cumsum)/reduce_window_sum | solution.py:51
  36.8 5.2 %convolution_bitcast_fusion = f32[4,2,8,160,160]{3,4,1,0,2:T(8,128)} fusion(bf16[3,8,128,2,128]{4,2,3,0,1:T(8,128)(2,1)S(1)} %copy.68, bf16[1,8,128,2,128]{4,2,3,0,1:T(8,128)(2,1)S(1)} %copy.67, f32[8,160]{1,0:T(8,128)S(1)} %get-tuple-element.38, f32[8,160]{1,0:T(8,128)S(1)} %get-tuple-element.37), kind=kOutput, calls=%fused_computation.8 | convolution fusion | flops 762118144 | bytes 8660992 | tf_op jit(solution)/shard_map/zty,fzybu->fbztu/dot_general | solution.py:87
  44.0 3.5 %fusion.15 = f32[1,2,8,160,160]{3,4,1,0,2:T(8,128)} fusion(f32[4,2,8,160,160]{3,4,1,0,2:T(8,128)} %convolution_bitcast_fusion), kind=kOutput, calls=%fused_computation.23 | output fusion | flops 2867200 | bytes 4259840 | tf_op jit(solution)/shard_map/jit(cumsum)/reduce_window_sum | solution.py:51
  56.2 5.6 %fusion.2 = f32[3,2,160,160]{2,3,1,0:T(8,128)} fusion(f32[4,2,8,160,160]{3,4,1,0,2:T(8,128)} %convolution_bitcast_fusion.2, f32[2,8,160,160]{2,3,0,1:T(8,128)S(1)} %multiply_bitcast_fusion.2), kind=kLoop, calls=%fused_computation.5 | loop fusion | flops 2304000 | bytes 7168000 | tf_op jit(solution)/shard_map/reduce_sum | solution.py:55
  64.9 5.6 %fusion.1 = f32[3,2,160,160]{2,3,1,0:T(8,128)} fusion(f32[4,2,8,160,160]{3,4,1,0,2:T(8,128)} %convolution_bitcast_fusion.1, f32[2,8,160,160]{2,3,0,1:T(8,128)S(1)} %multiply_bitcast_fusion.1), kind=kLoop, calls=%fused_computation.3 | loop fusion | flops 2304000 | bytes 7168000 | tf_op jit(solution)/shard_map/reduce_sum | solution.py:55
  73.7 4.5 %fusion = f32[3,2,160,160]{2,3,1,0:T(8,128)S(1)} fusion(f32[4,2,8,160,160]{3,4,1,0,2:T(8,128)} %convolution_bitcast_fusion, f32[2,8,160,160]{2,3,0,1:T(8,128)S(1)} %multiply_bitcast_fusion), kind=kLoop, calls=%fused_computation.1 | loop fusion | flops 2304000 | bytes 7168000 | tf_op jit(solution)/shard_map/reduce_sum | solution.py:55
  79.3 7.5 %dynamic_update_slice.21 = f32[4,176,304]{1,2,0:T(8,128)S(1)} dynamic-update-slice(f32[4,176,304]{1,2,0:T(8,128)S(1)} %broadcast.352.clone.2, f32[4,160,160]{1,2,0:T(8,128)} %fusion.32, s32[]{:T(128)} %constant.98.clone.1, s32[]{:T(128)S(6)} %select_n.161, s32[]{:T(128)S(6)} %select_n.162) | dynamic-update-slice | bytes 819204 | tf_op jit(solution)/shard_map/dynamic_update_slice | solution.py:99
  89.0 6.7 %dynamic_update_slice.22 = f32[1,4,176,304]{2,3,1,0:T(8,128)S(1)} dynamic-update-slice(f32[1,4,176,304]{2,3,1,0:T(8,128)S(1)} %bitcast.217, f32[1,4,160,160]{2,3,1,0:T(8,128)} %fusion.41, s32[]{:T(128)} %constant.98.clone.1, s32[]{:T(128)} %constant.98.clone.1, s32[]{:T(128)S(6)} %select_n.163, s32[]{:T(128)S(6)} %select_n.164) | dynamic-update-slice | bytes 819204 | tf_op jit(solution)/shard_map/dynamic_update_slice | solution.py:99
  97.6 7.6 %dynamic_update_slice.23 = f32[4,176,304]{1,2,0:T(8,128)S(1)} dynamic-update-slice(f32[4,176,304]{1,2,0:T(8,128)S(1)} %broadcast.352.clone.1, f32[4,160,160]{1,2,0:T(8,128)} %fusion.30, s32[]{:T(128)} %constant.98.clone.1, s32[]{:T(128)S(6)} %select_n.167, s32[]{:T(128)S(6)} %select_n.168) | dynamic-update-slice | bytes 819204 | tf_op jit(solution)/shard_map/dynamic_update_slice | solution.py:99
  107.4 6.6 %dynamic_update_slice.24 = f32[1,4,176,304]{2,3,1,0:T(8,128)S(1)} dynamic-update-slice(f32[1,4,176,304]{2,3,1,0:T(8,128)S(1)} %bitcast.218, f32[1,4,160,160]{2,3,1,0:T(8,128)} %fusion.38, s32[]{:T(128)} %constant.98.clone.1, s32[]{:T(128)} %constant.98.clone.1, s32[]{:T(128)S(6)} %select_n.169, s32[]{:T(128)S(6)} %select_n.170) | dynamic-update-slice | bytes 819204 | tf_op jit(solution)/shard_map/dynamic_update_slice | solution.py:99
  116.2 7.6 %dynamic_update_slice.25 = f32[4,176,304]{1,2,0:T(8,128)S(1)} dynamic-update-slice(f32[4,176,304]{1,2,0:T(8,128)S(1)} %broadcast.352.clone, f32[4,160,160]{1,2,0:T(8,128)} %fusion.28, s32[]{:T(128)} %constant.98.clone.1, s32[]{:T(128)S(6)} %select_n.173, s32[]{:T(128)S(6)} %select_n.174) | dynamic-update-slice | bytes 819204 | tf_op jit(solution)/shard_map/dynamic_update_slice | solution.py:99
  125.8 6.7 %dynamic_update_slice.26 = f32[1,4,176,304]{2,3,1,0:T(8,128)S(1)} dynamic-update-slice(f32[1,4,176,304]{2,3,1,0:T(8,128)S(1)} %bitcast.216, f32[1,4,160,160]{2,3,1,0:T(8,128)} %fusion.35, s32[]{:T(128)} %constant.98.clone.1, s32[]{:T(128)} %constant.98.clone.1, s32[]{:T(128)S(6)} %select_n.175, s32[]{:T(128)S(6)} %select_n.176) | dynamic-update-slice | bytes 819204 | tf_op jit(solution)/shard_map/dynamic_update_slice | solution.py:99
  139.9 2.9 %copy.73 = f32[3,4,24,304]{3,2,1,0:T(8,128)} copy(f32[3,4,24,304]{2,3,1,0:T(8,128)} %get-tuple-element.8) | data formatting | bytes 700416 | tf_op jit(solution)/shard_map/slice | solution.py:34
  144.8 7.0 %collective-permute-done = f32[3,4,24,304]{3,2,1,0:T(8,128)S(1)} collective-permute-done((f32[3,4,24,304]{3,2,1,0:T(8,128)S(1)}, f32[3,4,24,304]{3,2,1,0:T(8,128)S(1)}, u32[]{:S(2)}, u32[]{:S(2)}) %collective-permute-start) | collective-permute-done | bytes 350240 | tf_op jit(solution)/shard_map/ppermute | solution.py:31
  161.7 4.6 %collective-permute-done.2 = f32[3,4,224,24]{2,3,1,0:T(8,128)S(1)} collective-permute-done((f32[3,4,224,24]{2,3,1,0:T(8,128)}, f32[3,4,224,24]{2,3,1,0:T(8,128)S(1)}, u32[]{:S(2)}, u32[]{:S(2)}) %collective-permute-start.2) | collective-permute-done | bytes 258080 | tf_op jit(solution)/shard_map/ppermute | solution.py:31
  166.3 4.3 %pad_maximum_fusion = f32[3,4,224,352]{2,3,1,0:T(8,128)S(1)} fusion(f32[3,4,224,24]{2,3,1,0:T(8,128)S(1)} %collective-permute-done.3, f32[3,4,24,304]{2,3,1,0:T(8,128)} %copy.75, f32[1,4,176,304]{2,3,1,0:T(8,128)S(1)} %dynamic_update_slice.26, f32[1,4,176,304]{2,3,1,0:T(8,128)} %copy-done, f32[1,4,176,304]{2,3,1,0:T(8,128)S(1)} %dynamic_update_slice.22, ...), kind=kLoop, calls=%fused_computation.6 | loop fusion | flops 5677056 | bytes 7569408 | tf_op jit(solution)/shard_map/concatenate | solution.py:35
  175.7 18.1 %collective-permute-done.4 = f32[3,4,16,4,256]{4,1,3,2,0:T(4,128)S(1)} collective-permute-done((f32[3,4,16,4,256]{4,1,3,2,0:T(4,128)S(1)}, f32[3,4,16,4,256]{4,1,3,2,0:T(4,128)S(1)}, u32[]{:S(2)}, u32[]{:S(2)}) %collective-permute-start.4) | collective-permute-done | bytes 786464 | tf_op jit(solution)/shard_map/ppermute | solution.py:22
  196.2 3.1 %collective-permute-start.5 = (f32[3,4,16,2,256]{4,2,3,1,0:T(8,128)S(1)}, f32[3,4,16,2,256]{4,2,3,1,0:T(8,128)S(1)}, u32[]{:S(2)}, u32[]{:S(2)}) collective-permute-start(f32[3,4,16,2,256]{4,2,3,1,0:T(8,128)S(1)} %select_bitcast_fusion.1), channel_id=1, source_target_pairs={{0,64},{64,0},{32,96},{96,32},{128,192},{192,128},{160,224},{224,1... | collective-permute-start | bytes 1179656 | tf_op jit(solution)/shard_map/ppermute | solution.py:22
  199.2 18.3 %collective-permute-done.5 = f32[3,4,16,2,256]{4,2,3,1,0:T(8,128)S(1)} collective-permute-done((f32[3,4,16,2,256]{4,2,3,1,0:T(8,128)S(1)}, f32[3,4,16,2,256]{4,2,3,1,0:T(8,128)S(1)}, u32[]{:S(2)}, u32[]{:S(2)}) %collective-permute-start.5) | collective-permute-done | bytes 393248 | tf_op jit(solution)/shard_map/ppermute | solution.py:22
  217.9 6.6 %collective-permute-start.6 = (f32[3,4,16,1,256]{4,2,1,0,3:T(8,128)S(1)}, f32[3,4,16,1,256]{4,2,1,0,3:T(8,128)S(1)}, u32[]{:S(2)}, u32[]{:S(2)}) collective-permute-start(f32[3,4,16,1,256]{4,2,1,0,3:T(8,128)S(1)} %select_bitcast_fusion.2), channel_id=1, source_target_pairs={{0,128},{128,0},{32,160},{160,32},{64,192},{192,64},{96,224},{224,... | collective-permute-start | bytes 589832 | tf_op jit(solution)/shard_map/ppermute | solution.py:22
  224.5 7.9 %collective-permute-done.6 = f32[3,4,16,1,256]{4,2,1,0,3:T(8,128)S(1)} collective-permute-done((f32[3,4,16,1,256]{4,2,1,0,3:T(8,128)S(1)}, f32[3,4,16,1,256]{4,2,1,0,3:T(8,128)S(1)}, u32[]{:S(2)}, u32[]{:S(2)}) %collective-permute-start.6) | collective-permute-done | bytes 196640 | tf_op jit(solution)/shard_map/ppermute | solution.py:22
  (91 shorter events, 58.7 us)
Async XLA Ops:
  11.8 41.9 %copy-start.8 = (f32[2,160,160]{1,2,0:T(8,128)}, f32[2,160,160]{1,2,0:T(8,128)S(1)}, u32[]{:S(2)}) copy-start(f32[2,160,160]{1,2,0:T(8,128)S(1)} %slice_reduce_fusion.2) | copy-start | bytes 614404
  11.8 3.5 %copy-start.10 = (s32[3,2,1,1,2]{0,4,3,2,1:T(2,128)S(1)}, s32[3,2,1,1,2]{0,4,3,2,1:T(2,128)}, u32[]{:S(2)}) copy-start(s32[3,2,1,1,2]{0,4,3,2,1:T(2,128)} %param.6) | copy-start | bytes 148
  25.5 36.9 %copy-start.7 = (f32[2,160,160]{1,2,0:T(8,128)}, f32[2,160,160]{1,2,0:T(8,128)S(1)}, u32[]{:S(2)}) copy-start(f32[2,160,160]{1,2,0:T(8,128)S(1)} %slice_reduce_fusion.1) | copy-start | bytes 614404
  44.0 27.2 %copy-start.6 = (f32[2,160,160]{1,2,0:T(8,128)}, f32[2,160,160]{1,2,0:T(8,128)S(1)}, u32[]{:S(2)}) copy-start(f32[2,160,160]{1,2,0:T(8,128)S(1)} %slice_reduce_fusion) | copy-start | bytes 614404
  44.0 8.4 %copy-start.11 = (s32[3,1]{0,1:T(1,128)S(1)}, s32[3,1]{0,1:T(1,128)}, u32[]{:S(2)}) copy-start(s32[3,1]{0,1:T(1,128)} %param.7) | copy-start | bytes 40
  44.0 9.7 %copy-start.1 = (f32[1,2,8,160,160]{3,4,1,0,2:T(8,128)S(1)}, f32[1,2,8,160,160]{3,4,1,0,2:T(8,128)}, u32[]{:S(2)}) copy-start(f32[1,2,8,160,160]{3,4,1,0,2:T(8,128)} %fusion.19) | copy-start | bytes 4915204
  56.2 6.2 %copy-start.2 = (f32[1,2,8,160,160]{3,4,1,0,2:T(8,128)S(1)}, f32[1,2,8,160,160]{3,4,1,0,2:T(8,128)}, u32[]{:S(2)}) copy-start(f32[1,2,8,160,160]{3,4,1,0,2:T(8,128)} %fusion.17) | copy-start | bytes 4915204
  64.9 6.2 %copy-start.3 = (f32[1,2,8,160,160]{3,4,1,0,2:T(8,128)S(1)}, f32[1,2,8,160,160]{3,4,1,0,2:T(8,128)}, u32[]{:S(2)}) copy-start(f32[1,2,8,160,160]{3,4,1,0,2:T(8,128)} %fusion.15) | copy-start | bytes 4915204
  73.7 4.6 %copy-start.5 = (f32[3,2,160,160]{2,3,1,0:T(8,128)S(1)}, f32[3,2,160,160]{2,3,1,0:T(8,128)}, u32[]{:S(2)}) copy-start(f32[3,2,160,160]{2,3,1,0:T(8,128)} %fusion.2) | copy-start | bytes 1843204
  73.7 4.6 %copy-start.9 = (f32[2,160,160]{1,2,0:T(8,128)S(1)}, f32[2,160,160]{1,2,0:T(8,128)}, u32[]{:S(2)}) copy-start(f32[2,160,160]{1,2,0:T(8,128)} %copy-done.8) | copy-start | bytes 614404
  79.3 16.4 %copy-start.4 = (f32[3,2,160,160]{2,3,1,0:T(8,128)S(1)}, f32[3,2,160,160]{2,3,1,0:T(8,128)}, u32[]{:S(2)}) copy-start(f32[3,2,160,160]{2,3,1,0:T(8,128)} %fusion.1) | copy-start | bytes 1843204
  114.1 2.0 copy-start
  138.6 13.3 %collective-permute-start = (f32[3,4,24,304]{3,2,1,0:T(8,128)S(1)}, f32[3,4,24,304]{3,2,1,0:T(8,128)S(1)}, u32[]{:S(2)}, u32[]{:S(2)}) collective-permute-start(f32[3,4,24,304]{3,2,1,0:T(8,128)S(1)} %copy.72), channel_id=1, source_target_pairs={{0,8},{8,16},{16,24},{24,0},{1,9},{9,17},{17,25},{25,1},{2,10},{10... | collective-permute-start | bytes 1050632 | tf_op jit(solution)/shard_map/ppermute | solution.py:31
  142.8 12.1 %collective-permute-start.1 = (f32[3,4,24,304]{3,2,1,0:T(8,128)}, f32[3,4,24,304]{3,2,1,0:T(8,128)}, u32[]{:S(2)}, u32[]{:S(2)}) collective-permute-start(f32[3,4,24,304]{3,2,1,0:T(8,128)} %copy.73), channel_id=1, source_target_pairs={{8,0},{16,8},{24,16},{0,24},{9,1},{17,9},{25,17},{1,25},{10,2},{18... | collective-permute-start | bytes 1050632 | tf_op jit(solution)/shard_map/ppermute | solution.py:34
  159.9 6.4 %collective-permute-start.2 = (f32[3,4,224,24]{2,3,1,0:T(8,128)}, f32[3,4,224,24]{2,3,1,0:T(8,128)S(1)}, u32[]{:S(2)}, u32[]{:S(2)}) collective-permute-start(f32[3,4,224,24]{2,3,1,0:T(8,128)} %get-tuple-element.5), channel_id=1, source_target_pairs={{0,1},{1,2},{2,3},{3,4},{4,5},{5,6},{6,7},{7,0},{8,9},{9,10},{10,1... | collective-permute-start | bytes 774152 | tf_op jit(solution)/shard_map/ppermute | solution.py:31
  159.9 6.4 %collective-permute-start.3 = (f32[3,4,224,24]{2,3,1,0:T(8,128)S(1)}, f32[3,4,224,24]{2,3,1,0:T(8,128)S(1)}, u32[]{:S(2)}, u32[]{:S(2)}) collective-permute-start(f32[3,4,224,24]{2,3,1,0:T(8,128)S(1)} %get-tuple-element.6), channel_id=1, source_target_pairs={{1,0},{2,1},{3,2},{4,3},{5,4},{6,5},{7,6},{0,7},{9,8},{10,9},{11,1... | collective-permute-start | bytes 774152 | tf_op jit(solution)/shard_map/ppermute | solution.py:34
  170.6 0.7 copy-start.13
  171.3 1.2 copy-start.12
  173.9 19.9 %collective-permute-start.4 = (f32[3,4,16,4,256]{4,1,3,2,0:T(4,128)S(1)}, f32[3,4,16,4,256]{4,1,3,2,0:T(4,128)S(1)}, u32[]{:S(2)}, u32[]{:S(2)}) collective-permute-start(f32[3,4,16,4,256]{4,1,3,2,0:T(4,128)S(1)} %select_bitcast_fusion), channel_id=1, source_target_pairs={{0,32},{32,0},{64,96},{96,64},{128,160},{160,128},{192,224},{224,1... | collective-permute-start | bytes 2359304 | tf_op jit(solution)/shard_map/ppermute | solution.py:22
  196.2 21.4 %collective-permute-start.5 = (f32[3,4,16,2,256]{4,2,3,1,0:T(8,128)S(1)}, f32[3,4,16,2,256]{4,2,3,1,0:T(8,128)S(1)}, u32[]{:S(2)}, u32[]{:S(2)}) collective-permute-start(f32[3,4,16,2,256]{4,2,3,1,0:T(8,128)S(1)} %select_bitcast_fusion.1), channel_id=1, source_target_pairs={{0,64},{64,0},{32,96},{96,32},{128,192},{192,128},{160,224},{224,1... | collective-permute-start | bytes 1179656 | tf_op jit(solution)/shard_map/ppermute | solution.py:22
  217.9 14.5 %collective-permute-start.6 = (f32[3,4,16,1,256]{4,2,1,0,3:T(8,128)S(1)}, f32[3,4,16,1,256]{4,2,1,0,3:T(8,128)S(1)}, u32[]{:S(2)}, u32[]{:S(2)}) collective-permute-start(f32[3,4,16,1,256]{4,2,1,0,3:T(8,128)S(1)} %select_bitcast_fusion.2), channel_id=1, source_target_pairs={{0,128},{128,0},{32,160},{160,32},{64,192},{192,64},{96,224},{224,... | collective-permute-start | bytes 589832 | tf_op jit(solution)/shard_map/ppermute | solution.py:22
where the time goes:
time: 236 us; the launch traced here: 234 us
  local copies, waits for them, and re-layouts  63.8 us (27%)
  other arithmetic  62.9 us (27%)
  waiting for transfers between devices  57.2 us (24%)
  between operations  17.5 us (7%)
  starting transfers between devices  16.6 us (7%)
  matrix products  15.5 us (7%)
    ppermute x3, waiting for transfers between devices, partner(): return lax.ppermute(block, axis, route)  44.3 us
    dynamic_update_slice x6, local copies, waits for them, and re-layouts, render_view(): lax.dynamic_update_slice(canvas, current + shaded[:, brick_index], corner)  42.7 us
    reduce_sum x3, other arithmetic, integrate(): colors = jnp.sum(footprint[1:] * weight, axis=-3)  15.7 us
    dot_general x3, matrix products, render_view(): jnp.einsum('zty,fzybu->fbztu', row_weights, resampled, preferred_element_...  15.5 us
    ppermute x2, waiting for transfers between devices, extended(): lax.ppermute(lax.slice_in_dim(block, block.shape[dim] - width, None, axis...  11.6 us
    ppermute x3, starting transfers between devices, partner(): return lax.ppermute(block, axis, route)  11.5 us
    another operation x3, other arithmetic, integrate(): running = jnp.cumsum(extinction, axis=-3)  10.6 us
    another operation x4, other arithmetic, local(): jnp.stack([render_view(fields, view_index, offsets, band_orders[view_inde...  7.95 us
  transfers between devices with their start and end apart: 7, of which 6 were waited for; matrix products, arithmetic and copies ran while one was open for 2% of the time, Pallas kernels for 0%

commit v1 on v0

v1 whole, which is shorter than its diff:
```python
import functools

import jax
import jax.numpy as jnp
from jax import lax
from jax.experimental import pallas as pl
from jax.experimental.pallas import tpu as pltpu
from jax.sharding import PartitionSpec as P

MESH = pl.DeviceIdType.MESH
VIEWS = 3
MARGIN = 16
JIT = 8
SLICES = 8
LEN = 128
SHEAR_ROWS = (0.75, -0.5, 0.25)
SHEAR_COLS = (-0.25, 0.625, -0.875)
RIMS = tuple(
    -(-int(abs(a) * (MARGIN - 2) * (SLICES - 1) / SLICES + 1 + JIT) // 8) * 8 for a in SHEAR_ROWS
)
RIM = max(RIMS)
TALL = LEN + 2 * RIM
SLOT = 32

ROW_UP, ROW_DOWN, COL_LEFT, COL_RIGHT, UP_LEFT, UP_RIGHT, DOWN_LEFT, DOWN_RIGHT = range(8)


def shift_of(rate, z):
    return rate * (MARGIN - 2) / SLICES * (2.0 * z - (SLICES - 1))


def tent(distance):
    return jnp.maximum(0.0, 1.0 - jnp.abs(distance)).astype(jnp.bfloat16)


def kernel(
    sections, bands, stripes,
    density, emission, offsets, orders, out,
    foot, image, left, right,
    from_row, from_col, from_corner, sent, got_0, got_1, got_2,
    send_rim, recv_rim, send_depth, recv_depth,
):
    got = (got_0, got_1, got_2)
    me = lax.axis_index("depth")
    band = lax.axis_index("row")
    stripe = lax.axis_index("col")

    def place(drow, dcol):
        return {
            "row": lax.rem(band + drow + bands, bands),
            "col": lax.rem(stripe + dcol + stripes, stripes),
        }

    around = {
        ROW_UP: place(-1, 0), ROW_DOWN: place(1, 0), COL_LEFT: place(0, -1), COL_RIGHT: place(0, 1),
        UP_LEFT: place(-1, -1), UP_RIGHT: place(-1, 1), DOWN_LEFT: place(1, -1), DOWN_RIGHT: place(1, 1),
    }
    barrier = pltpu.get_barrier_semaphore()
    for device in around.values():
        pl.semaphore_signal(barrier, inc=1, device_id=device, device_id_type=MESH)
    for hop in range(1, sections):
        pl.semaphore_signal(
            barrier, inc=1, device_id={"depth": lax.rem(me + hop, sections)}, device_id_type=MESH
        )

    lane = lax.broadcasted_iota(jnp.int32, (LEN, 2 * LEN), 1)
    cell = lax.broadcasted_iota(jnp.int32, (LEN, 2 * LEN), 0)
    tail = lane - LEN
    nowhere = -4096
    column = (
        jnp.where(lane < LEN, lane, jnp.where(tail < SLOT, tail + LEN,
                  jnp.where(tail < 2 * SLOT, tail - 2 * SLOT, nowhere))),
        jnp.where(lane < LEN, lane, jnp.where(tail < 2 * SLOT, nowhere,
                  jnp.where(tail < 3 * SLOT, tail + LEN - 2 * SLOT, tail - LEN))),
    )
    col_base = [(c - cell).astype(jnp.float32) for c in column]
    tile_lane = lax.broadcasted_iota(jnp.int32, (8, LEN), 1)

    def resample(view):
        rim = RIMS[view]
        tall = LEN + 2 * rim
        row_base = (
            lax.broadcasted_iota(jnp.int32, (tall, LEN), 0) - rim
            - lax.broadcasted_iota(jnp.int32, (tall, LEN), 1)
        ).astype(jnp.float32)

        def slice_body(z, carry):
            zf = z.astype(jnp.float32)
            tails, row_weights = [], []
            for b in range(2):
                oy = offsets[view * 4 + b].astype(jnp.float32)
                ox = offsets[view * 4 + 2 + b].astype(jnp.float32)
                cols = slice(b * LEN, (b + 1) * LEN)
                cells = jnp.concatenate(
                    [density[z, :, cols]] + [emission[c, z, :, cols] for c in range(3)], 0
                )
                col_weights = tent(col_base[b] - (ox + shift_of(SHEAR_COLS[view], zf)))
                lines = jnp.dot(
                    cells, col_weights, preferred_element_type=jnp.float32
                ).astype(jnp.bfloat16)
                rw = tent(row_base - (oy + shift_of(SHEAR_ROWS[view], zf)))
                own = jnp.concatenate([lines[f * LEN:(f + 1) * LEN, :LEN] for f in range(4)], 1)
                tails.append(
                    jnp.concatenate([lines[f * LEN:(f + 1) * LEN, LEN:] for f in range(4)], 1)
                )
                row_weights.append(rw)
                prints = jnp.dot(rw, own, preferred_element_type=jnp.float32)
                for f in range(4):
                    foot[b, z, f, 0:tall, :] = prints[:, f * LEN:(f + 1) * LEN]
            prints = jnp.dot(
                jnp.concatenate(row_weights, 1), jnp.concatenate(tails, 0),
                preferred_element_type=jnp.float32,
            )
            for f in range(4):
                foot[2, z, f, 0:tall, :] = prints[:, f * LEN:(f + 1) * LEN]
            return carry

        lax.fori_loop(0, SLICES, slice_body, 0)

    def shade(view):
        rim = RIMS[view]
        tall = LEN + 2 * rim
        backward = orders[view]
        steps = [z + backward * (SLICES - 1 - 2 * z) for z in range(SLICES)]

        def integrate(region, rows):
            through = jnp.ones((8, LEN), jnp.float32)
            depth = jnp.zeros((8, LEN), jnp.float32)
            colors = [jnp.zeros((8, LEN), jnp.float32) for _ in range(3)]
            for z in steps:
                e = foot[region, z, 0, rows, :]
                after = through * jnp.exp(-e)
                weight = through - after
                through = after
                depth += e
                for c in range(3):
                    colors[c] += foot[region, z, 1 + c, rows, :] * weight
            return colors + [depth]

        def row_body(i, carry):
            rows = pl.ds(pl.multiple_of(i * 8, 8), 8)
            rims = integrate(2, rows)
            lefts = jnp.zeros((8, LEN), jnp.float32)
            rights = jnp.zeros((8, LEN), jnp.float32)
            for c in range(4):
                mine = jnp.where((tile_lane >= SLOT) & (tile_lane < 2 * SLOT), rims[c], 0.0)
                lefts += pltpu.roll(mine, (SLOT * c - SLOT) % LEN, 1)
                mine = jnp.where((tile_lane >= 2 * SLOT) & (tile_lane < 3 * SLOT), rims[c], 0.0)
                rights += pltpu.roll(mine, (SLOT * c - 2 * SLOT) % LEN, 1)
            left[view, rows, :] = lefts
            right[view, rows, :] = rights
            first = integrate(0, rows)
            for c in range(4):
                image[view, 0, c, rows, :] = first[c] + jnp.where(tile_lane >= 3 * SLOT, rims[c], 0.0)
            second = integrate(1, rows)
            for c in range(4):
                image[view, 1, c, rows, :] = second[c] + jnp.where(tile_lane < SLOT, rims[c], 0.0)
            return carry

        lax.fori_loop(0, tall // 8, row_body, 0)

    def rim_copies(view):
        rim = RIMS[view]
        top, mid, low = pl.ds(0, rim), pl.ds(rim, LEN), pl.ds(rim + LEN, rim)
        near = pl.ds(0, rim)
        moves = {
            ROW_UP: (image.at[view, :, :, top, :], from_row.at[view, 0, :, :, near, :]),
            ROW_DOWN: (image.at[view, :, :, low, :], from_row.at[view, 1, :, :, near, :]),
            COL_LEFT: (left.at[view, mid, :], from_col.at[view, 0]),
            COL_RIGHT: (right.at[view, mid, :], from_col.at[view, 1]),
            UP_LEFT: (left.at[view, top, :], from_corner.at[view, 0, near, :]),
            UP_RIGHT: (right.at[view, top, :], from_corner.at[view, 1, near, :]),
            DOWN_LEFT: (left.at[view, low, :], from_corner.at[view, 2, near, :]),
            DOWN_RIGHT: (right.at[view, low, :], from_corner.at[view, 3, near, :]),
        }
        return [
            pltpu.make_async_remote_copy(
                src_ref=src, dst_ref=dst,
                send_sem=send_rim.at[view, way], recv_sem=recv_rim.at[view, way],
                device_id=around[way], device_id_type=MESH,
            )
            for way, (src, dst) in moves.items()
        ]

    def fold(view):
        rim = RIMS[view]
        tiles = LEN // 8
        for i in range(tiles):
            rows = slice(rim + i * 8, rim + i * 8 + 8)
            here = slice(i * 8, i * 8 + 8)
            from_right = from_col[view, 0, here, :]
            from_left = from_col[view, 1, here, :]
            above = i * 8 < rim
            below = i * 8 >= LEN - rim
            if above:
                from_right += from_corner[view, 2, here, :]
                from_left += from_corner[view, 3, here, :]
            if below:
                lows = slice(i * 8 - (LEN - rim), i * 8 - (LEN - rim) + 8)
                from_right += from_corner[view, 0, lows, :]
                from_left += from_corner[view, 1, lows, :]
            for c in range(4):
                own = [image[view, b, c, rows, :] for b in range(2)]
                own[0] += jnp.where(
                    tile_lane < SLOT, pltpu.roll(from_left, (-SLOT * c) % LEN, 1), 0.0
                )
                own[1] += jnp.where(
                    tile_lane >= LEN - SLOT,
                    pltpu.roll(from_right, (LEN - SLOT - SLOT * c) % LEN, 1), 0.0,
                )
                for b in range(2):
                    if above:
                        own[b] += from_row[view, 1, b, c, here, :]
                    if below:
                        own[b] += from_row[view, 0, b, c, lows, :]
                    image[view, b, c, rows, :] = own[b]
        for k in range(sections):
            for c in range(4):
                for b in range(2):
                    sent[view, k, b, c] = image[
                        view, b, c, pl.ds(rim + k, LEN // sections, stride=sections), :
                    ]

    def depth_copies(view):
        copies = []
        for hop in range(1, sections):
            other = lax.rem(me + hop, sections)
            copies.append(
                pltpu.make_async_remote_copy(
                    src_ref=sent.at[view, other], dst_ref=got[view].at[hop],
                    send_sem=send_depth.at[view, hop], recv_sem=recv_depth.at[view, hop],
                    device_id={"depth": other}, device_id_type=MESH,
                )
            )
        return copies

    def composite(view):
        got[view][0] = sent[view, me]
        backward = orders[view]
        rows = LEN // sections
        for b in range(2):
            cols = slice(b * LEN, (b + 1) * LEN)
            through = jnp.ones((rows, LEN), jnp.float32)
            colors = [jnp.zeros((rows, LEN), jnp.float32) for _ in range(3)]
            for step in range(sections):
                slab = step + backward * (sections - 1 - 2 * step)
                slot = lax.rem(me - slab + sections, sections)
                for c in range(3):
                    colors[c] += got[view][slot, b, c] * through
                through = through * jnp.exp(-got[view][slot, b, 3])
            for c in range(3):
                out[view, c, :, cols] = colors[c]
            out[view, 3, :, cols] = through

    rim_sends, depth_sends = [], []
    for view in range(VIEWS):
        resample(view)
        shade(view)
        if view == 0:
            pl.semaphore_wait(barrier, 8 + sections - 1)
        rim_sends.append(rim_copies(view))
        for copy in rim_sends[view]:
            copy.start()
        if view > 0:
            for copy in rim_sends[view - 1]:
                copy.wait()
            fold(view - 1)
            depth_sends.append(depth_copies(view - 1))
            for copy in depth_sends[view - 1]:
                copy.start()
    for copy in rim_sends[VIEWS - 1]:
        copy.wait()
    fold(VIEWS - 1)
    depth_sends.append(depth_copies(VIEWS - 1))
    for copy in depth_sends[VIEWS - 1]:
        copy.start()
    for view in range(VIEWS):
        for copy in depth_sends[view]:
            copy.wait()
        composite(view)


def local(density, emission, offsets, view_order, sections, bands, stripes):
    rows, columns = LEN // sections, 2 * LEN
    vmem, smem = pl.BlockSpec(memory_space=pltpu.VMEM), pl.BlockSpec(memory_space=pltpu.SMEM)
    image = pl.pallas_call(
        functools.partial(kernel, sections, bands, stripes),
        out_shape=jax.ShapeDtypeStruct((VIEWS, 4, rows, columns), jnp.float32),
        in_specs=[vmem, vmem, smem, smem],
        out_specs=vmem,
        scratch_shapes=[
            pltpu.VMEM((3, SLICES, 4, TALL, LEN), jnp.float32),
            pltpu.VMEM((VIEWS, 2, 4, TALL, LEN), jnp.float32),
            pltpu.VMEM((VIEWS, TALL, LEN), jnp.float32),
            pltpu.VMEM((VIEWS, TALL, LEN), jnp.float32),
            pltpu.VMEM((VIEWS, 2, 2, 4, RIM, LEN), jnp.float32),
            pltpu.VMEM((VIEWS, 2, LEN, LEN), jnp.float32),
            pltpu.VMEM((VIEWS, 4, RIM, LEN), jnp.float32),
            pltpu.VMEM((VIEWS, sections, 2, 4, rows, LEN), jnp.float32),
            pltpu.VMEM((sections, 2, 4, rows, LEN), jnp.float32),
            pltpu.VMEM((sections, 2, 4, rows, LEN), jnp.float32),
            pltpu.VMEM((sections, 2, 4, rows, LEN), jnp.float32),
            pltpu.SemaphoreType.DMA((VIEWS, 8)),
            pltpu.SemaphoreType.DMA((VIEWS, 8)),
            pltpu.SemaphoreType.DMA((VIEWS, sections)),
            pltpu.SemaphoreType.DMA((VIEWS, sections)),
        ],
        compiler_params=pltpu.CompilerParams(
            collective_id=0, has_side_effects=True, vmem_limit_bytes=48 * 1024 * 1024
        ),
    )(density, emission, offsets.reshape(-1), view_order.reshape(-1))
    return image.reshape(VIEWS, 4, rows, 1, columns)


def solution(mesh):
    return jax.shard_map(
        functools.partial(
            local, sections=mesh.shape["depth"], bands=mesh.shape["row"], stripes=mesh.shape["col"]
        ),
        mesh=mesh,
        in_specs=(
            P("depth", "row", "col"),
            P(None, "depth", "row", "col"),
            P(None, None, "depth", "row", "col"),
            P(None, "row"),
        ),
        out_specs=P(None, None, "row", "depth", "col"),
        check_vma=False,
    )
```

time: 236 us -> 66.8 us (0.28)
  other arithmetic: 62.9 us -> 0 us
  Pallas kernels: 0 us -> 60.9 us
  local copies, waits for them, and re-layouts: 63.8 us -> 4.84 us
  waiting for transfers between devices: 57.2 us -> 0 us
  between operations: 17.5 us -> 0.01 us
  starting transfers between devices: 16.6 us -> 0 us
  matrix products: 15.5 us -> 0 us
    pallas_call x0 -> x1, Pallas kernels: none -> 60.9 us  [local(): pl.pallas_call(functools.partial(kernel, sections, bands, stripes), out_s...]
    ppermute x7 -> x0, waiting for transfers between devices: 57.2 us -> none  [the longest x3 44.3 us: partner(): return lax.ppermute(block, axis, route)]
    dynamic_update_slice x6 -> x0, local copies, waits for them, and re-layouts: 42.7 us -> none  [render_view(): lax.dynamic_update_slice(canvas, current + shaded[:, brick_index], corner)]
    reduce_sum x6 -> x0, other arithmetic: 21.6 us -> none  [the longest x3 15.7 us: integrate(): colors = jnp.sum(footprint[1:] * weight, axis=-3)]
    another operation x7 -> x0, other arithmetic: 18.5 us -> none  [the longest x3 10.6 us: integrate(): running = jnp.cumsum(extinction, axis=-3)]
    ppermute x7 -> x0, starting transfers between devices: 16.6 us -> none  [the longest x3 11.5 us: partner(): return lax.ppermute(block, axis, route)]
    dot_general x3 -> x0, matrix products: 15.5 us -> none  [render_view(): jnp.einsum('zty,fzybu->fbztu', row_weights, resampled, preferred_element_...]
    slice x7 -> x0, local copies, waits for them, and re-layouts: 9.47 us -> none  [the longest x2 4.55 us: extended(): lax.slice_in_dim(block, block.shape[dim] - width, None, axis=dim)]
  transfers between devices with their start and end apart: 7 -> 0, of which waited for: 6 -> 0; matrix products, arithmetic and copies ran while one was open for 2% -> 0% of each run, Pallas kernels for 0% -> 0%
where the time goes in v1:
time: 66.8 us; the launch traced here: 65.8 us
  Pallas kernels  60.9 us (91%)
  local copies, waits for them, and re-layouts  4.84 us (7%)
    pallas_call x1, Pallas kernels, local(): pl.pallas_call(functools.partial(kernel, sections, bands, stripes), out_s...  60.9 us
    unnamed x7, local copies, waits for them, and re-layouts  3.88 us

profile of v1, /device:TPU:6, one launch (start us, length us, event | category | flops | bytes accessed | tf_op | source)
XLA Modules:
  0.0 65.8 jit_solution(11766808951672105820)
XLA Ops:
  0.0 0.8 %copy.7 = s32[3,2,1,1,2]{4,1,0,3,2:T(2,128)S(1)} copy(s32[3,2,1,1,2]{0,4,3,2,1:T(2,128)} %param.6) | data formatting | bytes 96 | tf_op args[2]
  0.8 0.1 reshape.9.offsets
  0.9 0.0 copy-start
  0.9 1.4 %copy-done = bf16[3,8,128,256]{3,2,1,0:T(8,128)(2,1)S(1)} copy-done((bf16[3,8,128,256]{3,2,1,0:T(8,128)(2,1)S(1)}, bf16[3,8,128,256]{3,2,1,0:T(8,128)(2,1)}, u32[]{:S(2)}) %copy-start) | copy-done | bytes 1572888
  2.3 0.0 copy-start.1
  2.3 1.0 %copy-done.1 = bf16[8,128,256]{2,1,0:T(8,128)(2,1)S(1)} copy-done((bf16[8,128,256]{2,1,0:T(8,128)(2,1)S(1)}, bf16[8,128,256]{2,1,0:T(8,128)(2,1)}, u32[]{:S(2)}) %copy-start.1) | copy-done | bytes 524312
  3.3 0.0 copy-start.2
  3.3 0.7 copy-done.2
  4.0 60.9 %shard_map.46 = f32[3,4,16,256]{3,2,1,0:T(8,128)S(1)} custom-call(bf16[8,128,256]{2,1,0:T(8,128)(2,1)S(1)} %copy-done.1, bf16[3,8,128,256]{3,2,1,0:T(8,128)(2,1)S(1)} %copy-done, s32[12]{0:T(128)S(1)} %reshape.9.offsets, s32[3]{0:T(128)S(1)} %bitcast.5), custom_call_target="tpu_custom_call" | custom-call | tf_op jit(solution)/shard_map/pallas_call | solution.py:286
  64.9 0.9 %copy.8 = f32[3,4,16,1,256]{4,3,2,1,0:T(1,128)} copy(f32[3,4,16,1,256]{4,2,1,0,3:T(8,128)S(1)} %bitcast.4) | data formatting | bytes 393216 | tf_op jit(solution)/shard_map/reshape | solution.py:312
Async XLA Ops:
  0.9 1.4 %copy-start = (bf16[3,8,128,256]{3,2,1,0:T(8,128)(2,1)S(1)}, bf16[3,8,128,256]{3,2,1,0:T(8,128)(2,1)}, u32[]{:S(2)}) copy-start(bf16[3,8,128,256]{3,2,1,0:T(8,128)(2,1)} %emission.1) | copy-start | bytes 4718596
  2.3 1.0 %copy-start.1 = (bf16[8,128,256]{2,1,0:T(8,128)(2,1)S(1)}, bf16[8,128,256]{2,1,0:T(8,128)(2,1)}, u32[]{:S(2)}) copy-start(bf16[8,128,256]{2,1,0:T(8,128)(2,1)} %density.1) | copy-start | bytes 1572868
  3.3 0.7 copy-start.2

commit v2 on v1

--- a/solution.py
+++ b/solution.py
@@ -35,13 +35,22 @@
 
 def kernel(
     sections, bands, stripes,
-    density, emission, offsets, orders, out,
-    foot, image, left, right,
-    from_row, from_col, from_corner, sent, got_0, got_1, got_2,
-    send_rim, recv_rim, send_depth, recv_depth,
+    density_hbm, emission_hbm, offsets, orders, out,
+    density, emission, foot, image, left, right,
+    from_row, from_col, from_corner, sent, raw, got_0, got_1, got_2,
+    load_sem, send_rim, recv_rim, send_near, recv_near, send_far, recv_far,
 ):
+    loads = (
+        pltpu.make_async_copy(density_hbm, density, load_sem.at[0]),
+        pltpu.make_async_copy(emission_hbm, emission, load_sem.at[1]),
+    )
+    for load in loads:
+        load.start()
     got = (got_0, got_1, got_2)
     me = lax.axis_index("depth")
+    odd = lax.rem(me, 2)
+    sign = 1 - 2 * odd
+    partner = me + sign
     band = lax.axis_index("row")
     stripe = lax.axis_index("col")
 
@@ -88,8 +97,8 @@
             zf = z.astype(jnp.float32)
             tails, row_weights = [], []
             for b in range(2):
-                oy = offsets[view * 4 + b].astype(jnp.float32)
-                ox = offsets[view * 4 + 2 + b].astype(jnp.float32)
+                oy = offsets[view, 0, 0, 0, b].astype(jnp.float32)
+                ox = offsets[view, 1, 0, 0, b].astype(jnp.float32)
                 cols = slice(b * LEN, (b + 1) * LEN)
                 cells = jnp.concatenate(
                     [density[z, :, cols]] + [emission[c, z, :, cols] for c in range(3)], 0
@@ -115,12 +124,12 @@
                 foot[2, z, f, 0:tall, :] = prints[:, f * LEN:(f + 1) * LEN]
             return carry
 
-        lax.fori_loop(0, SLICES, slice_body, 0)
+        lax.fori_loop(0, SLICES, slice_body, 0, unroll=4)
 
     def shade(view):
         rim = RIMS[view]
         tall = LEN + 2 * rim
-        backward = orders[view]
+        backward = orders[view, 0]
         steps = [z + backward * (SLICES - 1 - 2 * z) for z in range(SLICES)]
 
         def integrate(region, rows):
@@ -215,80 +224,129 @@
                         own[b] += from_row[view, 0, b, c, lows, :]
                     image[view, b, c, rows, :] = own[b]
         for k in range(sections):
-            for c in range(4):
-                for b in range(2):
-                    sent[view, k, b, c] = image[
+            place_of = lax.rem(sign * (k - me) + sections, sections)
+            for b in range(2):
+                for c in range(4):
+                    part = image[
                         view, b, c, pl.ds(rim + k, LEN // sections, stride=sections), :
                     ]
-
-    def depth_copies(view):
-        copies = []
-        for hop in range(1, sections):
-            other = lax.rem(me + hop, sections)
-            copies.append(
-                pltpu.make_async_remote_copy(
-                    src_ref=sent.at[view, other], dst_ref=got[view].at[hop],
-                    send_sem=send_depth.at[view, hop], recv_sem=recv_depth.at[view, hop],
-                    device_id={"depth": other}, device_id_type=MESH,
-                )
+                    sent[view, place_of, b, c] = jnp.exp(-part) if c == 3 else part
+
+    def over(view, near, far):
+        mine_first = orders[view, 0] == odd
+        weight_near = jnp.where(mine_first, 1.0, far[3])
+        weight_far = jnp.where(mine_first, near[3], 1.0)
+        return [near[c] * weight_near + far[c] * weight_far for c in range(3)] + [near[3] * far[3]]
+
+    def near_copies(view):
+        return [
+            pltpu.make_async_remote_copy(
+                src_ref=sent.at[view, e], dst_ref=raw.at[view, e - 1],
+                send_sem=send_near.at[view, e - 1], recv_sem=recv_near.at[view, e - 1],
+                device_id={"depth": partner}, device_id_type=MESH,
             )
-        return copies
+            for e in (4, 3, 2, 1)
+        ]
+
+    def far_copy(view, e):
+        other = lax.rem(me - sign * (sections - e) + 2 * sections, sections)
+        slot = lax.rem(me // 2 - other // 2 + sections // 2, sections // 2)
+        return pltpu.make_async_remote_copy(
+            src_ref=sent.at[view, e], dst_ref=got[view].at[slot],
+            send_sem=send_far.at[view, e - 5], recv_sem=recv_far.at[view, slot],
+            device_id={"depth": other}, device_id_type=MESH,
+        )
+
+    def merge(view):
+        for e in (5, 6, 7):
+            near_sends[view][e - 5].wait_recv()
+            for b in range(2):
+                merged = over(
+                    view, [sent[view, e, b, c] for c in range(4)], [raw[view, 7 - (e - 1), b, c] for c in range(4)]
+                )
+                for c in range(4):
+                    sent[view, e, b, c] = merged[c]
+            far_sends[view].append(far_copy(view, e))
+            far_sends[view][-1].start()
+        near_sends[view][3].wait_recv()
+        for b in range(2):
+            merged = over(
+                view, [sent[view, 0, b, c] for c in range(4)], [raw[view, 0, b, c] for c in range(4)]
+            )
+            for c in range(4):
+                got[view][0, b, c] = merged[c]
 
     def composite(view):
-        got[view][0] = sent[view, me]
-        backward = orders[view]
+        backward = orders[view, 0]
+        pairs = sections // 2
+        for slot in range(1, pairs):
+            pltpu.make_async_remote_copy(
+                src_ref=sent.at[view, 5], dst_ref=got[view].at[slot],
+                send_sem=send_far.at[view, 0], recv_sem=recv_far.at[view, slot],
+                device_id={"depth": partner}, device_id_type=MESH,
+            ).wait_recv()
         rows = LEN // sections
         for b in range(2):
             cols = slice(b * LEN, (b + 1) * LEN)
             through = jnp.ones((rows, LEN), jnp.float32)
             colors = [jnp.zeros((rows, LEN), jnp.float32) for _ in range(3)]
-            for step in range(sections):
-                slab = step + backward * (sections - 1 - 2 * step)
-                slot = lax.rem(me - slab + sections, sections)
+            for step in range(pairs):
+                pair = step + backward * (pairs - 1 - 2 * step)
+                slot = lax.rem(pair - me // 2 + pairs, pairs)
                 for c in range(3):
                     colors[c] += got[view][slot, b, c] * through
-                through = through * jnp.exp(-got[view][slot, b, 3])
+                through = through * got[view][slot, b, 3]
             for c in range(3):
                 out[view, c, :, cols] = colors[c]
             out[view, 3, :, cols] = through
 
-    rim_sends, depth_sends = [], []
+    rim_sends, near_sends, far_sends = [], [], [[] for _ in range(VIEWS)]
+
+    def settle(view):
+        for copy in rim_sends[view]:
+            copy.wait()
+        fold(view)
+        near_sends.append(near_copies(view))
+        for copy in near_sends[view]:
+            copy.start()
+
+    for load in loads:
+        load.wait()
     for view in range(VIEWS):
         resample(view)
+        if view > 0:
+            settle(view - 1)
         shade(view)
         if view == 0:
             pl.semaphore_wait(barrier, 8 + sections - 1)
         rim_sends.append(rim_copies(view))
         for copy in rim_sends[view]:
             copy.start()
-        if view > 0:
-            for copy in rim_sends[view - 1]:
-                copy.wait()
-            fold(view - 1)
-            depth_sends.append(depth_copies(view - 1))
-            for copy in depth_sends[view - 1]:
-                copy.start()
-    for copy in rim_sends[VIEWS - 1]:
-        copy.wait()
-    fold(VIEWS - 1)
-    depth_sends.append(depth_copies(VIEWS - 1))
-    for copy in depth_sends[VIEWS - 1]:
-        copy.start()
+    merge(0)
+    settle(2)
+    merge(1)
+    composite(0)
+    merge(2)
+    composite(1)
+    composite(2)
     for view in range(VIEWS):
-        for copy in depth_sends[view]:
-            copy.wait()
-        composite(view)
+        for copy in near_sends[view] + far_sends[view]:
+            copy.wait_send()
 
 
 def local(density, emission, offsets, view_order, sections, bands, stripes):
     rows, columns = LEN // sections, 2 * LEN
-    vmem, smem = pl.BlockSpec(memory_space=pltpu.VMEM), pl.BlockSpec(memory_space=pltpu.SMEM)
+    vmem, smem, hbm = (
+        pl.BlockSpec(memory_space=space) for space in (pltpu.VMEM, pltpu.SMEM, pltpu.HBM)
+    )
     image = pl.pallas_call(
         functools.partial(kernel, sections, bands, stripes),
         out_shape=jax.ShapeDtypeStruct((VIEWS, 4, rows, columns), jnp.float32),
-        in_specs=[vmem, vmem, smem, smem],
+        in_specs=[hbm, hbm, smem, smem],
         out_specs=vmem,
         scratch_shapes=[
+            pltpu.VMEM(density.shape, density.dtype),
+            pltpu.VMEM(emission.shape, emission.dtype),
             pltpu.VMEM((3, SLICES, 4, TALL, LEN), jnp.float32),
             pltpu.VMEM((VIEWS, 2, 4, TALL, LEN), jnp.float32),
             pltpu.VMEM((VIEWS, TALL, LEN), jnp.float32),
@@ -297,18 +355,22 @@
             pltpu.VMEM((VIEWS, 2, LEN, LEN), jnp.float32),
             pltpu.VMEM((VIEWS, 4, RIM, LEN), jnp.float32),
             pltpu.VMEM((VIEWS, sections, 2, 4, rows, LEN), jnp.float32),
-            pltpu.VMEM((sections, 2, 4, rows, LEN), jnp.float32),
-            pltpu.VMEM((sections, 2, 4, rows, LEN), jnp.float32),
-            pltpu.VMEM((sections, 2, 4, rows, LEN), jnp.float32),
+            pltpu.VMEM((VIEWS, 4, 2, 4, rows, LEN), jnp.float32),
+            pltpu.VMEM((sections // 2, 2, 4, rows, LEN), jnp.float32),
+            pltpu.VMEM((sections // 2, 2, 4, rows, LEN), jnp.float32),
+            pltpu.VMEM((sections // 2, 2, 4, rows, LEN), jnp.float32),
+            pltpu.SemaphoreType.DMA((2,)),
             pltpu.SemaphoreType.DMA((VIEWS, 8)),
             pltpu.SemaphoreType.DMA((VIEWS, 8)),
-            pltpu.SemaphoreType.DMA((VIEWS, sections)),
-            pltpu.SemaphoreType.DMA((VIEWS, sections)),
+            pltpu.SemaphoreType.DMA((VIEWS, 4)),
+            pltpu.SemaphoreType.DMA((VIEWS, 4)),
+            pltpu.SemaphoreType.DMA((VIEWS, 4)),
+            pltpu.SemaphoreType.DMA((VIEWS, 4)),
         ],
         compiler_params=pltpu.CompilerParams(
-            collective_id=0, has_side_effects=True, vmem_limit_bytes=48 * 1024 * 1024
+            collective_id=0, has_side_effects=True, vmem_limit_bytes=60 * 1024 * 1024
         ),
-    )(density, emission, offsets.reshape(-1), view_order.reshape(-1))
+    )(density, emission, offsets, view_order)
     return image.reshape(VIEWS, 4, rows, 1, columns)
 
 

time: 66.8 us -> 59.3 us (0.89); the launches traced: 65.8 us -> 59.1 us
  Pallas kernels: 60.9 us -> 54.6 us
    pallas_call x1, Pallas kernels: 60.9 us -> 54.6 us  [local(): pl.pallas_call(functools.partial(kernel, sections, bands, stripes), out_s...]
    unnamed x7 -> x2, local copies, waits for them, and re-layouts: 3.88 us -> 2.65 us
    reshape x1, local copies, waits for them, and re-layouts: 0.88 us -> 1.81 us  [local(): return image.reshape(VIEWS, 4, rows, 1, columns)]
where the time goes in v2:
time: 59.3 us; the launch traced here: 59.1 us
  Pallas kernels  54.6 us (92%)
  local copies, waits for them, and re-layouts  4.46 us (8%)
    pallas_call x1, Pallas kernels, local(): pl.pallas_call(functools.partial(kernel, sections, bands, stripes), out_s...  54.6 us
    unnamed x2, local copies, waits for them, and re-layouts  2.65 us
    reshape x1, local copies, waits for them, and re-layouts, local(): return image.reshape(VIEWS, 4, rows, 1, columns)  1.81 us

profile of v2, /device:TPU:6, one launch (start us, length us, event | category | flops | bytes accessed | tf_op | source)
XLA Modules:
  0.0 59.1 jit_solution(11590365629572593233)
XLA Ops:
  0.0 1.3 %copy.6.orders = s32[3,1]{1,0:T(4,128)} copy(s32[3,1]{0,1:T(1,128)} %param.7) | data formatting | bytes 24 | tf_op args[3]
  1.3 1.3 %copy.5.offsets = s32[3,2,1,1,2]{4,3,2,1,0:T(1,128)} copy(s32[3,2,1,1,2]{0,4,3,2,1:T(2,128)} %param.6) | data formatting | bytes 96 | tf_op args[2]
  2.7 54.6 %shard_map.46 = f32[3,4,16,256]{3,2,1,0:T(8,128)} custom-call(bf16[8,128,256]{2,1,0:T(8,128)(2,1)} %density_hbm.1, bf16[3,8,128,256]{3,2,1,0:T(8,128)(2,1)} %emission_hbm.1, s32[3,2,1,1,2]{4,3,2,1,0:T(1,128)} %copy.5.offsets, s32[3,1]{1,0:T(4,128)} %copy.6.orders), custom_call_target="tpu_custom_call" | custom-call | tf_op jit(solution)/shard_map/pallas_call | solution.py:342
  57.3 1.8 %copy.7 = f32[3,4,16,1,256]{4,3,2,1,0:T(1,128)} copy(f32[3,4,16,1,256]{4,2,1,0,3:T(8,128)} %bitcast.1) | data formatting | bytes 393216 | tf_op jit(solution)/shard_map/reshape | solution.py:374

commit v3 on v2

--- a/solution.py
+++ b/solution.py
@@ -95,10 +95,10 @@
 
         def slice_body(z, carry):
             zf = z.astype(jnp.float32)
-            tails, row_weights = [], []
+            owns, tails, row_weights = [], [], []
             for b in range(2):
-                oy = offsets[view, 0, 0, 0, b].astype(jnp.float32)
-                ox = offsets[view, 1, 0, 0, b].astype(jnp.float32)
+                oy = offsets[0, b, view].astype(jnp.float32)
+                ox = offsets[1, b, view].astype(jnp.float32)
                 cols = slice(b * LEN, (b + 1) * LEN)
                 cells = jnp.concatenate(
                     [density[z, :, cols]] + [emission[c, z, :, cols] for c in range(3)], 0
@@ -107,29 +107,28 @@
                 lines = jnp.dot(
                     cells, col_weights, preferred_element_type=jnp.float32
                 ).astype(jnp.bfloat16)
-                rw = tent(row_base - (oy + shift_of(SHEAR_ROWS[view], zf)))
-                own = jnp.concatenate([lines[f * LEN:(f + 1) * LEN, :LEN] for f in range(4)], 1)
-                tails.append(
-                    jnp.concatenate([lines[f * LEN:(f + 1) * LEN, LEN:] for f in range(4)], 1)
-                )
-                row_weights.append(rw)
-                prints = jnp.dot(rw, own, preferred_element_type=jnp.float32)
-                for f in range(4):
-                    foot[b, z, f, 0:tall, :] = prints[:, f * LEN:(f + 1) * LEN]
+                row_weights.append(tent(row_base - (oy + shift_of(SHEAR_ROWS[view], zf))))
+                owns.append([lines[f * LEN:(f + 1) * LEN, :LEN] for f in range(4)])
+                tails.append([lines[f * LEN:(f + 1) * LEN, LEN:] for f in range(4)])
+            none = jnp.zeros((LEN, 4 * LEN), jnp.bfloat16)
+            above = jnp.concatenate(owns[0] + [none] + tails[0], 1)
+            below = jnp.concatenate([none] + owns[1] + tails[1], 1)
             prints = jnp.dot(
-                jnp.concatenate(row_weights, 1), jnp.concatenate(tails, 0),
+                jnp.concatenate(row_weights, 1), jnp.concatenate([above, below], 0),
                 preferred_element_type=jnp.float32,
             )
-            for f in range(4):
-                foot[2, z, f, 0:tall, :] = prints[:, f * LEN:(f + 1) * LEN]
+            for region in range(3):
+                for f in range(4):
+                    at = (region * 4 + f) * LEN
+                    foot[region, z, f, 0:tall, :] = prints[:, at:at + LEN]
             return carry
 
-        lax.fori_loop(0, SLICES, slice_body, 0, unroll=4)
+        lax.fori_loop(0, SLICES, slice_body, 0, unroll=8)
 
     def shade(view):
         rim = RIMS[view]
         tall = LEN + 2 * rim
-        backward = orders[view, 0]
+        backward = orders[view]
         steps = [z + backward * (SLICES - 1 - 2 * z) for z in range(SLICES)]
 
         def integrate(region, rows):
@@ -233,7 +232,7 @@
                     sent[view, place_of, b, c] = jnp.exp(-part) if c == 3 else part
 
     def over(view, near, far):
-        mine_first = orders[view, 0] == odd
+        mine_first = orders[view] == odd
         weight_near = jnp.where(mine_first, 1.0, far[3])
         weight_far = jnp.where(mine_first, near[3], 1.0)
         return [near[c] * weight_near + far[c] * weight_far for c in range(3)] + [near[3] * far[3]]
@@ -277,7 +276,7 @@
                 got[view][0, b, c] = merged[c]
 
     def composite(view):
-        backward = orders[view, 0]
+        backward = orders[view]
         pairs = sections // 2
         for slot in range(1, pairs):
             pltpu.make_async_remote_copy(
@@ -287,7 +286,7 @@
             ).wait_recv()
         rows = LEN // sections
         for b in range(2):
-            cols = slice(b * LEN, (b + 1) * LEN)
+            lines = pl.ds(b, rows, stride=2)
             through = jnp.ones((rows, LEN), jnp.float32)
             colors = [jnp.zeros((rows, LEN), jnp.float32) for _ in range(3)]
             for step in range(pairs):
@@ -297,8 +296,8 @@
                     colors[c] += got[view][slot, b, c] * through
                 through = through * got[view][slot, b, 3]
             for c in range(3):
-                out[view, c, :, cols] = colors[c]
-            out[view, 3, :, cols] = through
+                out[view, c, lines, :] = colors[c]
+            out[view, 3, lines, :] = through
 
     rim_sends, near_sends, far_sends = [], [], [[] for _ in range(VIEWS)]
 
@@ -312,16 +311,20 @@
 
     for load in loads:
         load.wait()
-    for view in range(VIEWS):
+    def render(view):
         resample(view)
-        if view > 0:
-            settle(view - 1)
         shade(view)
         if view == 0:
             pl.semaphore_wait(barrier, 8 + sections - 1)
         rim_sends.append(rim_copies(view))
         for copy in rim_sends[view]:
             copy.start()
+
+    render(0)
+    render(1)
+    settle(0)
+    render(2)
+    settle(1)
     merge(0)
     settle(2)
     merge(1)
@@ -341,7 +344,7 @@
     )
     image = pl.pallas_call(
         functools.partial(kernel, sections, bands, stripes),
-        out_shape=jax.ShapeDtypeStruct((VIEWS, 4, rows, columns), jnp.float32),
+        out_shape=jax.ShapeDtypeStruct((VIEWS, 4, 2 * rows, LEN), jnp.float32),
         in_specs=[hbm, hbm, smem, smem],
         out_specs=vmem,
         scratch_shapes=[
@@ -370,7 +373,10 @@
         compiler_params=pltpu.CompilerParams(
             collective_id=0, has_side_effects=True, vmem_limit_bytes=60 * 1024 * 1024
         ),
-    )(density, emission, offsets, view_order)
+    )(
+        density, emission,
+        offsets.transpose(1, 2, 3, 4, 0).reshape(2, 2, VIEWS), view_order.reshape(-1),
+    )
     return image.reshape(VIEWS, 4, rows, 1, columns)
 
 

time: 59.3 us -> 50.8 us (0.86)
  Pallas kernels: 54.6 us -> 48.9 us
  local copies, waits for them, and re-layouts: 4.46 us -> 1.74 us
    pallas_call x1, Pallas kernels: 54.6 us -> 48.9 us  [local(): pl.pallas_call(functools.partial(kernel, sections, bands, stripes), out_s...]
    reshape x1 -> x0, local copies, waits for them, and re-layouts: 1.81 us -> none  [local(): return image.reshape(VIEWS, 4, rows, 1, columns)]
    unnamed x2 -> x1, local copies, waits for them, and re-layouts: 2.65 us -> 1.74 us
where the time goes in v3:
time: 50.8 us; the launch traced here: 50.7 us
  Pallas kernels  48.9 us (96%)
  local copies, waits for them, and re-layouts  1.74 us (3%)
    pallas_call x1, Pallas kernels, local(): pl.pallas_call(functools.partial(kernel, sections, bands, stripes), out_s...  48.9 us
    unnamed x1, local copies, waits for them, and re-layouts  1.74 us

profile of v3, /device:TPU:6, one launch (start us, length us, event | category | flops | bytes accessed | tf_op | source)
XLA Modules:
  0.0 50.7 jit_solution(14114962593524188720)
XLA Ops:
  0.0 48.9 %shard_map.46 = f32[3,4,32,128]{3,2,1,0:T(8,128)} custom-call(bf16[8,128,256]{2,1,0:T(8,128)(2,1)} %density_hbm.1, bf16[3,8,128,256]{3,2,1,0:T(8,128)(2,1)} %emission_hbm.1, s32[2,2,3]{2,1,0:T(2,128)} %bitcast.6, s32[3]{0:T(128)} %bitcast.7), custom_call_target="tpu_custom_call" | custom-call | tf_op jit(solution)/shard_map/pallas_call | solution.py:345
  48.9 1.7 %copy.7 = f32[3,4,16,1,256]{4,3,2,1,0:T(1,128)} copy(f32[3,4,16,1,256]{4,3,2,1,0:T(1,128)} %bitcast.5) | data formatting | bytes 393216

commit v4 on v3

--- a/solution.py
+++ b/solution.py
@@ -172,14 +172,14 @@
         top, mid, low = pl.ds(0, rim), pl.ds(rim, LEN), pl.ds(rim + LEN, rim)
         near = pl.ds(0, rim)
         moves = {
+            UP_LEFT: (left.at[view, top, :], from_corner.at[view, 0, near, :]),
+            UP_RIGHT: (right.at[view, top, :], from_corner.at[view, 1, near, :]),
+            DOWN_LEFT: (left.at[view, low, :], from_corner.at[view, 2, near, :]),
+            DOWN_RIGHT: (right.at[view, low, :], from_corner.at[view, 3, near, :]),
             ROW_UP: (image.at[view, :, :, top, :], from_row.at[view, 0, :, :, near, :]),
             ROW_DOWN: (image.at[view, :, :, low, :], from_row.at[view, 1, :, :, near, :]),
             COL_LEFT: (left.at[view, mid, :], from_col.at[view, 0]),
             COL_RIGHT: (right.at[view, mid, :], from_col.at[view, 1]),
-            UP_LEFT: (left.at[view, top, :], from_corner.at[view, 0, near, :]),
-            UP_RIGHT: (right.at[view, top, :], from_corner.at[view, 1, near, :]),
-            DOWN_LEFT: (left.at[view, low, :], from_corner.at[view, 2, near, :]),
-            DOWN_RIGHT: (right.at[view, low, :], from_corner.at[view, 3, near, :]),
         }
         return [
             pltpu.make_async_remote_copy(
@@ -299,13 +299,13 @@
                 out[view, c, lines, :] = colors[c]
             out[view, 3, lines, :] = through
 
-    rim_sends, near_sends, far_sends = [], [], [[] for _ in range(VIEWS)]
+    rim_sends, near_sends, far_sends = {}, {}, [[] for _ in range(VIEWS)]
 
     def settle(view):
         for copy in rim_sends[view]:
             copy.wait()
         fold(view)
-        near_sends.append(near_copies(view))
+        near_sends[view] = near_copies(view)
         for copy in near_sends[view]:
             copy.start()
 
@@ -314,24 +314,24 @@
     def render(view):
         resample(view)
         shade(view)
-        if view == 0:
+        if view == 2:
             pl.semaphore_wait(barrier, 8 + sections - 1)
-        rim_sends.append(rim_copies(view))
+        rim_sends[view] = rim_copies(view)
         for copy in rim_sends[view]:
             copy.start()
 
+    render(2)
+    render(1)
+    settle(2)
     render(0)
-    render(1)
+    settle(1)
+    merge(2)
     settle(0)
-    render(2)
-    settle(1)
+    merge(1)
+    composite(2)
     merge(0)
-    settle(2)
-    merge(1)
+    composite(1)
     composite(0)
-    merge(2)
-    composite(1)
-    composite(2)
     for view in range(VIEWS):
         for copy in near_sends[view] + far_sends[view]:
             copy.wait_send()

time: 50.8 us -> 49.6 us (0.976)
  Pallas kernels: 48.9 us -> 47.6 us
    pallas_call x1, Pallas kernels: 48.9 us -> 47.6 us  [local(): pl.pallas_call(functools.partial(kernel, sections, bands, stripes), out_s...]
where the time goes in v4:
time: 49.6 us; the launch traced here: 49.4 us
  Pallas kernels  47.6 us (96%)
  local copies, waits for them, and re-layouts  1.74 us (4%)
    pallas_call x1, Pallas kernels, local(): pl.pallas_call(functools.partial(kernel, sections, bands, stripes), out_s...  47.6 us
    unnamed x1, local copies, waits for them, and re-layouts  1.74 us

profile of v4, /device:TPU:6, one launch (start us, length us, event | category | flops | bytes accessed | tf_op | source)
XLA Modules:
  0.0 49.4 jit_solution(16768992817776824413)
XLA Ops:
  0.0 47.6 %shard_map.46 = f32[3,4,32,128]{3,2,1,0:T(8,128)} custom-call(bf16[8,128,256]{2,1,0:T(8,128)(2,1)} %density_hbm.1, bf16[3,8,128,256]{3,2,1,0:T(8,128)(2,1)} %emission_hbm.1, s32[2,2,3]{2,1,0:T(2,128)} %bitcast.6, s32[3]{0:T(128)} %bitcast.7), custom_call_target="tpu_custom_call" | custom-call | tf_op jit(solution)/shard_map/pallas_call | solution.py:345
  47.6 1.7 %copy.7 = f32[3,4,16,1,256]{4,3,2,1,0:T(1,128)} copy(f32[3,4,16,1,256]{4,3,2,1,0:T(1,128)} %bitcast.5) | data formatting | bytes 393216

commit v5 on v4

--- a/solution.py
+++ b/solution.py
@@ -371,11 +371,16 @@
             pltpu.SemaphoreType.DMA((VIEWS, 4)),
         ],
         compiler_params=pltpu.CompilerParams(
-            collective_id=0, has_side_effects=True, vmem_limit_bytes=60 * 1024 * 1024
+            collective_id=0, has_side_effects=True, vmem_limit_bytes=50 * 1024 * 1024
         ),
     )(
-        density, emission,
-        offsets.transpose(1, 2, 3, 4, 0).reshape(2, 2, VIEWS), view_order.reshape(-1),
+        *(
+            pltpu.with_memory_space_constraint(x, pltpu.HBM)
+            for x in (
+                density, emission,
+                offsets.transpose(1, 2, 3, 4, 0).reshape(2, 2, VIEWS), view_order.reshape(-1),
+            )
+        )
     )
     return image.reshape(VIEWS, 4, rows, 1, columns)
 

time: 49.6 us -> 47.9 us (0.966)
  local copies, waits for them, and re-layouts: 1.74 us -> 0.68 us
  Pallas kernels: 47.6 us -> 46.9 us
    unnamed x1, local copies, waits for them, and re-layouts: 1.74 us -> 0.68 us
    pallas_call x1, Pallas kernels: 47.6 us -> 46.9 us  [local(): pl.pallas_call(functools.partial(kernel, sections, bands, stripes), out_s...]
where the time goes in v5:
time: 47.9 us; the launch traced here: 47.6 us
  Pallas kernels  46.9 us (98%)
  local copies, waits for them, and re-layouts  0.68 us (1%)
    pallas_call x1, Pallas kernels, local(): pl.pallas_call(functools.partial(kernel, sections, bands, stripes), out_s...  46.9 us

profile of v5, /device:TPU:6, one launch (start us, length us, event | category | flops | bytes accessed | tf_op | source)
XLA Modules:
  0.0 47.6 jit_solution(9120343530838042656)
XLA Ops:
  0.0 46.9 %shard_map.46 = f32[3,4,32,128]{3,2,1,0:T(8,128)S(1)} custom-call(bf16[8,128,256]{2,1,0:T(8,128)(2,1)} %density_hbm.1, bf16[3,8,128,256]{3,2,1,0:T(8,128)(2,1)} %emission_hbm.1, s32[2,2,3]{2,1,0:T(2,128)} %bitcast.6, s32[3]{0:T(128)} %bitcast.7), custom_call_target="tpu_custom_call" | custom-call | tf_op jit(solution)/shard_map/pallas_call | solution.py:345
  47.0 0.7 %copy.7 = f32[3,4,16,1,256]{4,3,2,1,0:T(1,128)} copy(f32[3,4,16,1,256]{4,3,2,1,0:T(1,128)S(1)} %bitcast.5) | data formatting | bytes 393216

commit v6 on v5

--- a/solution.py
+++ b/solution.py
@@ -40,12 +40,15 @@
     from_row, from_col, from_corner, sent, raw, got_0, got_1, got_2,
     load_sem, send_rim, recv_rim, send_near, recv_near, send_far, recv_far,
 ):
-    loads = (
-        pltpu.make_async_copy(density_hbm, density, load_sem.at[0]),
-        pltpu.make_async_copy(emission_hbm, emission, load_sem.at[1]),
-    )
-    for load in loads:
-        load.start()
+    loads = []
+    for part in range(SLICES // 2):
+        zs = slice(2 * part, 2 * part + 2)
+        loads.append((
+            pltpu.make_async_copy(density_hbm.at[zs], density.at[zs], load_sem.at[0, part]),
+            pltpu.make_async_copy(emission_hbm.at[:, zs], emission.at[:, zs], load_sem.at[1, part]),
+        ))
+        for load in loads[part]:
+            load.start()
     got = (got_0, got_1, got_2)
     me = lax.axis_index("depth")
     odd = lax.rem(me, 2)
@@ -85,7 +88,7 @@
     col_base = [(c - cell).astype(jnp.float32) for c in column]
     tile_lane = lax.broadcasted_iota(jnp.int32, (8, LEN), 1)
 
-    def resample(view):
+    def resample(view, first):
         rim = RIMS[view]
         tall = LEN + 2 * rim
         row_base = (
@@ -93,8 +96,8 @@
             - lax.broadcasted_iota(jnp.int32, (tall, LEN), 1)
         ).astype(jnp.float32)
 
-        def slice_body(z, carry):
-            zf = z.astype(jnp.float32)
+        def slice_body(z):
+            zf = jnp.float32(z)
             owns, tails, row_weights = [], [], []
             for b in range(2):
                 oy = offsets[0, b, view].astype(jnp.float32)
@@ -121,9 +124,12 @@
                 for f in range(4):
                     at = (region * 4 + f) * LEN
                     foot[region, z, f, 0:tall, :] = prints[:, at:at + LEN]
-            return carry
-
-        lax.fori_loop(0, SLICES, slice_body, 0, unroll=8)
+
+        for z in range(SLICES):
+            if first and z % 2 == 0:
+                for load in loads[z // 2]:
+                    load.wait()
+            slice_body(z)
 
     def shade(view):
         rim = RIMS[view]
@@ -309,10 +315,8 @@
         for copy in near_sends[view]:
             copy.start()
 
-    for load in loads:
-        load.wait()
     def render(view):
-        resample(view)
+        resample(view, view == 2)
         shade(view)
         if view == 2:
             pl.semaphore_wait(barrier, 8 + sections - 1)
@@ -328,8 +332,8 @@
     merge(2)
     settle(0)
     merge(1)
+    merge(0)
     composite(2)
-    merge(0)
     composite(1)
     composite(0)
     for view in range(VIEWS):
@@ -362,7 +366,7 @@
             pltpu.VMEM((sections // 2, 2, 4, rows, LEN), jnp.float32),
             pltpu.VMEM((sections // 2, 2, 4, rows, LEN), jnp.float32),
             pltpu.VMEM((sections // 2, 2, 4, rows, LEN), jnp.float32),
-            pltpu.SemaphoreType.DMA((2,)),
+            pltpu.SemaphoreType.DMA((2, SLICES // 2)),
             pltpu.SemaphoreType.DMA((VIEWS, 8)),
             pltpu.SemaphoreType.DMA((VIEWS, 8)),
             pltpu.SemaphoreType.DMA((VIEWS, 4)),

time: 47.9 us -> 47.9 us (level)
  no operation moved by 1% of the time
where the time goes in v6:
time: 47.9 us; the launch traced here: 47.7 us
  Pallas kernels  47 us (98%)
  local copies, waits for them, and re-layouts  0.68 us (1%)
    pallas_call x1, Pallas kernels, local(): pl.pallas_call(functools.partial(kernel, sections, bands, stripes), out_s...  47 us

profile of v6, /device:TPU:6, one launch (start us, length us, event | category | flops | bytes accessed | tf_op | source)
XLA Modules:
  0.0 47.7 jit_solution(2782647747515934040)
XLA Ops:
  0.0 47.0 %shard_map.46 = f32[3,4,32,128]{3,2,1,0:T(8,128)S(1)} custom-call(bf16[8,128,256]{2,1,0:T(8,128)(2,1)} %density_hbm.1, bf16[3,8,128,256]{3,2,1,0:T(8,128)(2,1)} %emission_hbm.1, s32[2,2,3]{2,1,0:T(2,128)} %bitcast.6, s32[3]{0:T(128)} %bitcast.7), custom_call_target="tpu_custom_call" | custom-call | tf_op jit(solution)/shard_map/pallas_call | solution.py:349
  47.0 0.7 %copy.7 = f32[3,4,16,1,256]{4,3,2,1,0:T(1,128)} copy(f32[3,4,16,1,256]{4,3,2,1,0:T(1,128)S(1)} %bitcast.5) | data formatting | bytes 393216

commit v7 on v5

--- a/solution.py
+++ b/solution.py
@@ -20,6 +20,7 @@
 )
 RIM = max(RIMS)
 TALL = LEN + 2 * RIM
+LOG2_E = 1.4426950408889634
 SLOT = 32
 
 ROW_UP, ROW_DOWN, COL_LEFT, COL_RIGHT, UP_LEFT, UP_RIGHT, DOWN_LEFT, DOWN_RIGHT = range(8)
@@ -137,7 +138,7 @@
             colors = [jnp.zeros((8, LEN), jnp.float32) for _ in range(3)]
             for z in steps:
                 e = foot[region, z, 0, rows, :]
-                after = through * jnp.exp(-e)
+                after = through * jnp.exp2(e * -LOG2_E)
                 weight = through - after
                 through = after
                 depth += e

time: 47.9 us -> 48.6 us (1.015)
  Pallas kernels: 46.9 us -> 47.8 us
    pallas_call x1, Pallas kernels: 46.9 us -> 47.8 us  [local(): pl.pallas_call(functools.partial(kernel, sections, bands, stripes), out_s...]
where the time goes in v7:
time: 48.6 us; the launch traced here: 48.5 us
  Pallas kernels  47.8 us (98%)
  local copies, waits for them, and re-layouts  0.68 us (1%)
    pallas_call x1, Pallas kernels, local(): pl.pallas_call(functools.partial(kernel, sections, bands, stripes), out_s...  47.8 us

profile of v7, /device:TPU:6, one launch (start us, length us, event | category | flops | bytes accessed | tf_op | source)
XLA Modules:
  0.0 48.5 jit_solution(8372868096415848776)
XLA Ops:
  0.0 47.8 %shard_map.46 = f32[3,4,32,128]{3,2,1,0:T(8,128)S(1)} custom-call(bf16[8,128,256]{2,1,0:T(8,128)(2,1)} %density_hbm.1, bf16[3,8,128,256]{3,2,1,0:T(8,128)(2,1)} %emission_hbm.1, s32[2,2,3]{2,1,0:T(2,128)} %bitcast.6, s32[3]{0:T(128)} %bitcast.7), custom_call_target="tpu_custom_call" | custom-call | tf_op jit(solution)/shard_map/pallas_call | solution.py:346
  47.8 0.7 %copy.7 = f32[3,4,16,1,256]{4,3,2,1,0:T(1,128)} copy(f32[3,4,16,1,256]{4,3,2,1,0:T(1,128)S(1)} %bitcast.5) | data formatting | bytes 393216
